TPU v7x, 32 devices: a whole 2x2x4 slice. The times are simulated.
32 devices in a mesh: dp: 4 (over x, core), expert: 8 (over z, y).
Axes of the slice: x: 2, y: 2, z: 4, core: 2. Of those that a mesh axis runs over, the one named last changes fastest.
Arguments:
- tokens: bfloat16 [256, 4096], P(('dp', 'expert')), may hold values from -6 to 6
- expert_ids: int32 [256, 8], P(('dp', 'expert')), may hold values from 0 to 31, all different within a row; in each aligned block of 8 rows (0 to 7, 8 to 15, ...) at most 4 rows name the same one
- gate_weights: float32 [256, 8], P(('dp', 'expert')), may hold values from 0.1 to 1
- gate_weight: bfloat16 [4096, 14336], P('dp', 'expert'), may hold values from -0.09375 to 0.09375
- up_weight: bfloat16 [4096, 14336], P('dp', 'expert'), may hold values from -0.09375 to 0.09375
- down_weight: bfloat16 [14336, 4096], P('expert', 'dp'), may hold values from -0.125 to 0.125
- expert_gain: float32 [4, 14336], P('dp', 'expert'), may hold values from 0.5 to 2
Outputs:
- mixed: bfloat16 [256, 4096], P(('dp', 'expert'))
Inputs may be any that keep to these rules, and one draw needn't show every extreme that they name: `expert_ids`: each row names 8 different experts. Among the 8 rows of one device no expert is named more than 4 times, a bound that some block reaches.
All inputs are finite; a program needn't handle non-finite values.
Results may differ from a plain program's by a relative error of at most 0.0055.
Values may be sent and summed in bfloat16 or wider, within the bound.
A program may use at most 128 MiB of HBM per device.

v0:
```python
import jax
import jax.numpy as jnp
from jax import lax
from jax.sharding import PartitionSpec as P

FF = 14336
EH = 1792


def slot_table(expert_ids, segments, capacity):
    tok_rows, top_count = expert_ids.shape
    flat_ids = expert_ids.reshape(-1)
    route_order = jnp.arange(flat_ids.shape[0], dtype=jnp.int32)
    earlier = (flat_ids[:, None] == flat_ids[None, :]) & (
        route_order[None, :] < route_order[:, None]
    )
    rank_in = jnp.sum(earlier.astype(jnp.int32), axis=1)
    copy_index = flat_ids // segments
    segment_index = flat_ids % segments
    group_index = copy_index * segments + segment_index
    return (group_index * capacity + rank_in).reshape(tok_rows, top_count)


def dispatch(tokens, position, slot_count):
    targets = jnp.arange(slot_count, dtype=jnp.int32)
    onehot = jnp.any(targets[:, None, None] == position[None, :, :], axis=2).astype(jnp.bfloat16)
    return jnp.dot(onehot, tokens, preferred_element_type=jnp.float32).astype(jnp.bfloat16)


def expert_block(routed, gate_weight, up_weight, down_weight, expert_gain):

    def add_rows(piece):
        return jnp.dot(routed, piece, preferred_element_type=jnp.float32)

    gate_sum = add_rows(lax.all_gather(gate_weight, "dp", axis=0, tiled=True))
    up_sum = add_rows(lax.all_gather(up_weight, "dp", axis=0, tiled=True))
    hidden = (jax.nn.silu(gate_sum) * up_sum * expert_gain).astype(jnp.bfloat16)
    partial_value = jnp.dot(
        hidden,
        lax.all_gather(down_weight, "dp", axis=1, tiled=True),
        preferred_element_type=jnp.float32,
    )
    return partial_value.astype(jnp.bfloat16)


def body(tokens, expert_ids, gate_weights, gate_weight, up_weight, down_weight, expert_gain):
    copies = lax.axis_size("dp")
    owners = lax.axis_size("expert")
    segments = FF // EH
    quarters = owners // segments
    tok_rows, top_count = expert_ids.shape
    model_width = tokens.shape[1]
    experts = copies * segments
    capacity = max(2, (2 * tok_rows * top_count + experts - 1) // experts)
    slot_count = experts * capacity
    position = slot_table(expert_ids, segments, capacity)
    buffer = dispatch(tokens, position, slot_count)
    sectioned = buffer.reshape(copies, segments, capacity, model_width)
    arrived = lax.all_to_all(sectioned, "dp", split_axis=0, concat_axis=2, tiled=True)
    spread = jnp.broadcast_to(
        arrived.reshape(segments, 1, copies * capacity, model_width),
        (segments, quarters, copies * capacity, model_width),
    )
    spread = spread.reshape(owners, copies * capacity, model_width)
    rows_in = lax.all_to_all(spread, "expert", split_axis=0, concat_axis=1, tiled=True)
    partial_value = expert_block(
        rows_in.reshape(-1, model_width), gate_weight, up_weight, down_weight, expert_gain
    )
    returned = lax.all_to_all(
        partial_value.reshape(1, owners * copies * capacity, model_width),
        "expert",
        split_axis=1,
        concat_axis=0,
        tiled=True,
    )
    summed = jnp.sum(
        returned.reshape(segments, quarters, copies * capacity, model_width).astype(jnp.float32),
        axis=1,
    )
    summed = summed.astype(jnp.bfloat16)
    at_home = lax.all_to_all(
        summed.reshape(1, segments, copies * capacity, model_width),
        "dp",
        split_axis=2,
        concat_axis=0,
        tiled=True,
    )
    results = at_home.reshape(slot_count, model_width)
    picked = jnp.take(results, position.reshape(-1), axis=0).reshape(
        tok_rows, top_count, model_width
    )
    mixed = jnp.sum(gate_weights[:, :, None] * picked.astype(jnp.float32), axis=1)
    return mixed.astype(jnp.bfloat16)


def solution(mesh):
    in_specs = (
        P(("dp", "expert"), None),
        P(("dp", "expert"), None),
        P(("dp", "expert"), None),
        P("dp", "expert"),
        P("dp", "expert"),
        P("expert", "dp"),
        P("dp", "expert"),
    )
    out_specs = P(("dp", "expert"), None)
    return jax.shard_map(body, mesh=mesh, in_specs=in_specs, out_specs=out_specs, check_vma=False)
```

profile of v0, /device:TPU:0, one launch (start us, length us, event | category | flops | bytes accessed | tf_op | source)
XLA Modules:
  0.0 390.4 jit_solution(17198120846166784655)
XLA Ops:
  6.5 0.0 copy-start
  6.5 0.0 copy-start.3
  6.5 0.0 all-gather.4.cloned.1.call-start
  6.5 0.7 all-gather.4.cloned.1.call-update
  7.3 0.0 all-gather.6.cloned.1.call-start
  7.3 0.7 all-gather.6.cloned.1.call-update
  8.0 0.0 all-gather.8.cloned.1.call-start
  8.1 0.7 all-gather.8.cloned.1.call-update
  8.7 0.8 reshape.204
  9.5 0.2 convert_reduce_fusion
  9.7 0.1 reduce_sum.27
  9.8 0.7 compare_and_fusion
  10.5 0.1 fusion.6
  10.6 0.0 copy-done
  10.6 0.5 convolution_convert_fusion.1
  11.1 0.4 reshape.205
  11.5 0.6 copy.24
  12.1 24.4 %all_to_all.51 = bf16[4,8,4,4096]{3,1,2,0:T(8,128)(2,1)S(1)} all-to-all(bf16[4,8,4,4096]{3,1,2,0:T(8,128)(2,1)S(1)} %copy.24), channel_id=1, replica_groups=mesh['dp'=4,'expert'=8] {'dp'}, dimensions={0} | all-to-all | bytes 2097152 | tf_op jit(solution)/shard_map/all_to_all | solution.py:59
  36.5 1.6 copy.25
  38.1 6.2 %all-to-all-start.1 = ((bf16[8,16,4096]{2,1,0:T(8,128)(2,1)}), bf16[8,16,4096]{2,1,0:T(8,128)(2,1)S(1)}, u32[]{:S(2)}, u32[]{:S(2)}) async-start(bf16[8,16,4096]{2,1,0:T(8,128)(2,1)} %copy.25), calls=%async_computation.1 | async-start | bytes 2097152 | tf_op jit(solution)/shard_map/all_to_all | solution.py:65
  44.3 0.0 copy-done.3
  44.3 25.3 %all-to-all-done.1 = bf16[8,16,4096]{2,1,0:T(8,128)(2,1)S(1)} async-done(((bf16[8,16,4096]{2,1,0:T(8,128)(2,1)}), bf16[8,16,4096]{2,1,0:T(8,128)(2,1)S(1)}, u32[]{:S(2)}, u32[]{:S(2)}) %all-to-all-start.1) | async-done | bytes 1048608 | tf_op jit(solution)/shard_map/all_to_all | solution.py:65
  69.6 41.7 %all-gather.4.cloned.1.call-done = bf16[4096,1792]{1,0:T(8,128)(2,1)} async-done(((bf16[1024,1792]{1,0:T(8,128)(2,1)}), bf16[4096,1792]{1,0:T(8,128)(2,1)}) %all-gather.4.cloned.1.call-update) | async-done | bytes 14680080 | tf_op jit(solution)/shard_map/all_gather | solution.py:35
  111.3 7.2 %fusion.19 = f32[128,1792]{1,0:T(8,128)S(1)} fusion(bf16[128,4096]{1,0:T(8,128)(2,1)S(1)} %bitcast.36, bf16[4096,1792]{1,0:T(8,128)(2,1)} %all-gather.4.cloned.1.call-done), kind=kOutput, calls=%fused_computation.45 | convolution fusion | flops 1879048192 | bytes 16646144 | tf_op jit(solution)/shard_map/dot_general | solution.py:33
  118.5 88.7 %all-gather.6.cloned.1.call-done = bf16[4096,1792]{1,0:T(8,128)(2,1)} async-done(((bf16[1024,1792]{1,0:T(8,128)(2,1)}), bf16[4096,1792]{1,0:T(8,128)(2,1)}) %all-gather.6.cloned.1.call-update) | async-done | bytes 14680080 | tf_op jit(solution)/shard_map/all_gather | solution.py:36
  207.2 95.6 %all-gather.8.cloned.1.call-done = bf16[1792,4096]{1,0:T(8,128)(2,1)} async-done(((bf16[1792,1024]{1,0:T(8,128)(2,1)}), bf16[1792,4096]{1,0:T(8,128)(2,1)}) %all-gather.8.cloned.1.call-update) | async-done | bytes 14680080 | tf_op jit(solution)/shard_map/all_gather | solution.py:40
  302.8 0.0 copy-start.1
  302.8 13.8 %fusion = bf16[1,128,4096]{2,1,0:T(8,128)(2,1)S(1)} fusion(bf16[1792,4096]{1,0:T(8,128)(2,1)} %all-gather.8.cloned.1.call-done, bf16[128,4096]{1,0:T(8,128)(2,1)S(1)} %bitcast.37, bf16[4096,1792]{1,0:T(8,128)(2,1)} %all-gather.6.cloned.1.call-done, f32[128,1792]{1,0:T(8,128)S(1)} %fusion.19, f32[1792]{0:T(1024)S(1)} %reduce), kind=kOutput, calls=%fused_computation.3 | convolution fusion | flops 3760226304 | bytes 32381952 | tf_op jit(solution)/shard_map/dot_general | solution.py:38
  316.6 0.0 copy-start.2
  316.7 0.0 copy-start.4
  316.7 2.4 copy.33
  319.0 0.5 broadcast.207
  319.6 7.2 %reduce.1 = bf16[128,4096]{1,0:T(8,128)(2,1)S(1)} reduce(bf16[128,1,4096]{2,1,0:T(2,128)(2,1)S(1)} %bitcast.39, bf16[]{:T(256)} %broadcast.207), dimensions={1}, to_apply=%bitcast.35.reduce_sub_computation | reduce | bytes 2097154
  326.8 0.8 reshape.219
  327.6 31.5 %all_to_all.52 = bf16[8,2,32768]{2,1,0:T(2,128)(2,1)S(1)} all-to-all(bf16[8,2,32768]{2,1,0:T(2,128)(2,1)S(1)} %reshape.219), channel_id=1, replica_groups=mesh['dp'=4,'expert'=8] {'expert'}, dimensions={0} | all-to-all | bytes 2097152 | tf_op jit(solution)/shard_map/all_to_all | solution.py:69
  359.1 1.0 reshape.220
  360.1 1.1 copy.29
  361.3 1.5 copy.27
  362.8 3.5 all-to-all-start.3
  366.3 0.0 copy-done.2
  366.4 0.1 reshape.209
  366.5 14.3 %all-to-all-done.3 = bf16[1,8,16,4096]{3,1,0,2:T(8,128)(2,1)S(1)} async-done(((bf16[1,8,16,4096]{3,1,0,2:T(8,128)(2,1)}), bf16[1,8,16,4096]{3,1,0,2:T(8,128)(2,1)S(1)}, u32[]{:S(2)}, u32[]{:S(2)}) %all-to-all-start.3) | async-done | bytes 1048608 | tf_op jit(solution)/shard_map/all_to_all | solution.py:81
  380.8 0.8 copy.32
  381.6 0.3 reshape.208
  381.9 0.9 gather_fusion
  382.8 0.0 copy-done.4
  382.8 1.1 multiply_reduce_fusion
  383.8 0.0 copy-done.1
  (3 shorter events, 0.0 us)
Async XLA Ops:
  6.5 4.1 %copy-start = (bf16[8,4096]{1,0:T(8,128)(2,1)S(1)}, bf16[8,4096]{1,0:T(8,128)(2,1)}, u32[]{:S(2)}) copy-start(bf16[8,4096]{1,0:T(8,128)(2,1)} %param.7) | copy-start | bytes 196612
  6.5 37.7 %copy-start.3 = (f32[1,1792]{1,0:T(1,128)S(1)}, f32[1,1792]{1,0:T(1,128)}, u32[]{:S(2)}) copy-start(f32[1,1792]{1,0:T(1,128)} %param.13) | copy-start | bytes 21508
  6.5 104.8 %all-gather.4.cloned.1.call-start = ((), (), s32[]{:S(2)}) async-start(), calls=%async_computation.4 | async-start | bytes 18350080 | tf_op jit(solution)/shard_map/all_gather | solution.py:35
  7.3 200.0 %all-gather.6.cloned.1.call-start = ((), (), s32[]{:S(2)}) async-start(), calls=%async_computation.5 | async-start | bytes 18350080 | tf_op jit(solution)/shard_map/all_gather | solution.py:36
  8.0 294.8 %all-gather.8.cloned.1.call-start = ((), (), s32[]{:S(2)}) async-start(), calls=%async_computation.6 | async-start | bytes 18350080 | tf_op jit(solution)/shard_map/all_gather | solution.py:40
  38.1 31.5 %all-to-all-start.1 = ((bf16[8,16,4096]{2,1,0:T(8,128)(2,1)}), bf16[8,16,4096]{2,1,0:T(8,128)(2,1)S(1)}, u32[]{:S(2)}, u32[]{:S(2)}) async-start(bf16[8,16,4096]{2,1,0:T(8,128)(2,1)} %copy.25), calls=%async_computation.1 | async-start | bytes 2097152 | tf_op jit(solution)/shard_map/all_to_all | solution.py:65
  302.8 81.0 %copy-start.1 = (bf16[8,4096]{1,0:T(8,128)(2,1)S(1)}, bf16[8,4096]{1,0:T(8,128)(2,1)}, u32[]{:S(2)}) copy-start(bf16[8,4096]{1,0:T(8,128)(2,1)} %param.7) | copy-start | bytes 196612
  316.6 49.7 %copy-start.2 = (s32[8,8]{1,0:T(8,128)S(1)}, s32[8,8]{1,0:T(8,128)}, u32[]{:S(2)}) copy-start(s32[8,8]{1,0:T(8,128)} %param.8) | copy-start | bytes 772
  316.7 66.1 %copy-start.4 = (f32[8,8]{1,0:T(8,128)S(1)}, f32[8,8]{1,0:T(8,128)}, u32[]{:S(2)}) copy-start(f32[8,8]{1,0:T(8,128)} %param.9) | copy-start | bytes 772
  362.8 18.0 %all-to-all-start.3 = ((bf16[1,8,16,4096]{3,1,0,2:T(8,128)(2,1)}), bf16[1,8,16,4096]{3,1,0,2:T(8,128)(2,1)S(1)}, u32[]{:S(2)}, u32[]{:S(2)}) async-start(bf16[1,8,16,4096]{3,1,0,2:T(8,128)(2,1)} %copy.27), calls=%async_computation.3 | async-start | bytes 2097152 | tf_op jit(solution)/shard_map/all_to_all | solution.py:81
Sparse Core Ops, SparseCore 0:
  8.9 102.3 all-gather.3
  112.8 94.3 all-gather.5
  208.8 94.0 all-gather.7
where the time goes:
time: 391 us; the launch traced here: 390 us
  waiting for transfers between devices  268 us (69%)
  blocking collectives  55.9 us (14%)
  matrix products  21.5 us (5%)
  between operations  13.3 us (3%)
  local copies, waits for them, and re-layouts  12.9 us (3%)
  starting transfers between devices  9.76 us (2%)
  other arithmetic  9.34 us (2%)
    all_gather x1, waiting for transfers between devices, expert_block(): lax.all_gather(down_weight, 'dp', axis=1, tiled=True)  95.6 us
    all_gather x1, waiting for transfers between devices, expert_block(): up_sum = add_rows(lax.all_gather(up_weight, 'dp', axis=0, tiled=True))  88.7 us
    all_gather x1, waiting for transfers between devices, expert_block(): gate_sum = add_rows(lax.all_gather(gate_weight, 'dp', axis=0, tiled=True))  41.7 us
    all_to_all x1, blocking collectives, body(): lax.all_to_all(partial_value.reshape(1, owners * copies * capacity, model...  31.5 us
    all_to_all x1, waiting for transfers between devices, body(): lax.all_to_all(spread, 'expert', split_axis=0, concat_axis=1, tiled=True)  25.3 us
    all_to_all x1, blocking collectives, body(): lax.all_to_all(sectioned, 'dp', split_axis=0, concat_axis=2, tiled=True)  24.4 us
    all_to_all x1, waiting for transfers between devices, body(): lax.all_to_all(summed.reshape(1, segments, copies * capacity, model_width...  14.3 us
    dot_general x1, matrix products, expert_block(): jnp.dot(hidden, lax.all_gather(down_weight, 'dp', axis=1, tiled=True), pr...  13.8 us
  transfers between devices with their start and end apart: 5, of which 5 were waited for; matrix products, arithmetic and copies ran while one was open for 3% of the time, Pallas kernels for 0%

commit v1 on v0

--- a/solution.py
+++ b/solution.py
@@ -5,6 +5,17 @@
 
 FF = 14336
 EH = 1792
+
+
+def cut_along(value, dim, size):
+    before, after = (value.shape[:dim], value.shape[dim + 1 :])
+    return jnp.moveaxis(value.reshape(*before, size, -1, *after), dim, 0)
+
+
+def in_order(blocks, dim):
+    blocks = jnp.moveaxis(blocks, 0, dim)
+    shape = blocks.shape
+    return blocks.reshape(*shape[:dim], shape[dim] * shape[dim + 1], *shape[dim + 2 :])
 
 
 def slot_table(expert_ids, segments, capacity):
@@ -78,13 +89,15 @@
         axis=1,
     )
     summed = summed.astype(jnp.bfloat16)
-    at_home = lax.all_to_all(
-        summed.reshape(1, segments, copies * capacity, model_width),
-        "dp",
-        split_axis=2,
-        concat_axis=0,
-        tiled=True,
-    )
+    x = summed.reshape(1, segments, copies * capacity, model_width)
+    size, index = (lax.axis_size("dp"), lax.axis_index("dp"))
+    pieces = cut_along(x, 2, size)
+    outs = [pieces[index]]
+    for step in range(1, size):
+        sent = pieces[index ^ step]
+        outs.append(lax.ppermute(sent, "dp", [(i, i ^ step) for i in range(size)]))
+    pieces = jnp.stack(outs)[index ^ jnp.arange(size)]
+    at_home = in_order(pieces, 0)
     results = at_home.reshape(slot_count, model_width)
     picked = jnp.take(results, position.reshape(-1), axis=0).reshape(
         tok_rows, top_count, model_width

time: 391 us -> 393 us (level)
  blocking collectives: 55.9 us -> 24.4 us
  waiting for transfers between devices: 268 us -> 290 us
  local copies, waits for them, and re-layouts: 12.9 us -> 18.8 us
  starting transfers between devices: 9.76 us -> 14 us
    all_to_all x1 -> x0, blocking collectives: 31.5 us -> none  [body(): lax.all_to_all(partial_value.reshape(1, owners * copies * capacity, model...]
    all_to_all x1, waiting for transfers between devices: 14.3 us -> 26.1 us  [body(): lax.all_to_all(partial_value.reshape(1, owners * copies * capacity, model...]
    ppermute x0 -> x3, waiting for transfers between devices: none -> 10.8 us  [body(): outs.append(lax.ppermute(sent, 'dp', [(i, i ^ step) for i in range(size)]))]
    all_to_all x1, local copies, waits for them, and re-layouts: 1.55 us -> 6.21 us  [body(): lax.all_to_all(partial_value.reshape(1, owners * copies * capacity, model...]
  transfers between devices with their start and end apart: 5 -> 8, of which waited for: 5 -> 7; matrix products, arithmetic and copies ran while one was open for 3% -> 3% of each run, Pallas kernels for 0% -> 0%
where the time goes in v1:
time: 393 us; the launch traced here: 392 us
  waiting for transfers between devices  290 us (74%)
  blocking collectives  24.4 us (6%)
  matrix products  21.5 us (5%)
  local copies, waits for them, and re-layouts  18.8 us (5%)
  starting transfers between devices  14 us (4%)
  between operations  13.3 us (3%)
  other arithmetic  10.3 us (3%)
    all_gather x1, waiting for transfers between devices, expert_block(): lax.all_gather(down_weight, 'dp', axis=1, tiled=True)  95.6 us
    all_gather x1, waiting for transfers between devices, expert_block(): up_sum = add_rows(lax.all_gather(up_weight, 'dp', axis=0, tiled=True))  88.7 us
    all_gather x1, waiting for transfers between devices, expert_block(): gate_sum = add_rows(lax.all_gather(gate_weight, 'dp', axis=0, tiled=True))  41.7 us
    all_to_all x1, waiting for transfers between devices, body(): lax.all_to_all(partial_value.reshape(1, owners * copies * capacity, model...  26.1 us
    all_to_all x1, waiting for transfers between devices, body(): lax.all_to_all(spread, 'expert', split_axis=0, concat_axis=1, tiled=True)  25.3 us
    all_to_all x1, blocking collectives, body(): lax.all_to_all(sectioned, 'dp', split_axis=0, concat_axis=2, tiled=True)  24.4 us
    dot_general x1, matrix products, expert_block(): jnp.dot(hidden, lax.all_gather(down_weight, 'dp', axis=1, tiled=True), pr...  13.8 us
    ppermute x3, waiting for transfers between devices, body(): outs.append(lax.ppermute(sent, 'dp', [(i, i ^ step) for i in range(size)]))  10.8 us
  transfers between devices with their start and end apart: 8, of which 7 were waited for; matrix products, arithmetic and copies ran while one was open for 3% of the time, Pallas kernels for 0%

profile of v1, /device:TPU:0, one launch (start us, length us, event | category | flops | bytes accessed | tf_op | source)
XLA Modules:
  0.0 392.5 jit_solution(5722571389339369443)
XLA Ops:
  6.5 0.7 all-gather.4.cloned.1.call-update
  7.3 0.0 all-gather.6.cloned.1.call-start
  7.3 0.7 all-gather.6.cloned.1.call-update
  8.0 0.0 all-gather.8.cloned.1.call-start
  8.1 0.7 all-gather.8.cloned.1.call-update
  8.7 0.8 reshape.226
  9.5 0.2 convert_reduce_fusion
  9.7 0.1 reduce_sum.27
  9.8 0.7 compare_and_fusion
  10.5 0.1 fusion.6
  10.6 0.0 copy-done
  10.6 0.5 convolution_convert_fusion.1
  11.1 0.4 reshape.227
  11.5 0.6 copy.17
  12.1 24.4 %all_to_all.33 = bf16[4,8,4,4096]{3,1,2,0:T(8,128)(2,1)S(1)} all-to-all(bf16[4,8,4,4096]{3,1,2,0:T(8,128)(2,1)S(1)} %copy.17), channel_id=1, replica_groups=mesh['dp'=4,'expert'=8] {'dp'}, dimensions={0} | all-to-all | bytes 2097152 | tf_op jit(solution)/shard_map/all_to_all | solution.py:70
  36.5 1.6 copy.18
  38.1 6.2 %all-to-all-start.1 = ((bf16[8,16,4096]{2,1,0:T(8,128)(2,1)}), bf16[8,16,4096]{2,1,0:T(8,128)(2,1)S(1)}, u32[]{:S(2)}, u32[]{:S(2)}) async-start(bf16[8,16,4096]{2,1,0:T(8,128)(2,1)} %copy.18), calls=%async_computation.1 | async-start | bytes 2097152 | tf_op jit(solution)/shard_map/all_to_all | solution.py:76
  44.3 25.3 %all-to-all-done.1 = bf16[8,16,4096]{2,1,0:T(8,128)(2,1)S(1)} async-done(((bf16[8,16,4096]{2,1,0:T(8,128)(2,1)}), bf16[8,16,4096]{2,1,0:T(8,128)(2,1)S(1)}, u32[]{:S(2)}, u32[]{:S(2)}) %all-to-all-start.1) | async-done | bytes 1048608 | tf_op jit(solution)/shard_map/all_to_all | solution.py:76
  69.6 41.7 %all-gather.4.cloned.1.call-done = bf16[4096,1792]{1,0:T(8,128)(2,1)} async-done(((bf16[1024,1792]{1,0:T(8,128)(2,1)}), bf16[4096,1792]{1,0:T(8,128)(2,1)}) %all-gather.4.cloned.1.call-update) | async-done | bytes 14680080 | tf_op jit(solution)/shard_map/all_gather | solution.py:46
  111.3 7.2 %fusion.20 = f32[128,1792]{1,0:T(8,128)S(1)} fusion(bf16[128,4096]{1,0:T(8,128)(2,1)S(1)} %bitcast.45, bf16[4096,1792]{1,0:T(8,128)(2,1)} %all-gather.4.cloned.1.call-done), kind=kOutput, calls=%fused_computation.54 | convolution fusion | flops 1879048192 | bytes 16646144 | tf_op jit(solution)/shard_map/dot_general | solution.py:44
  118.5 0.0 copy-start.2
  118.6 88.7 %all-gather.6.cloned.1.call-done = bf16[4096,1792]{1,0:T(8,128)(2,1)} async-done(((bf16[1024,1792]{1,0:T(8,128)(2,1)}), bf16[4096,1792]{1,0:T(8,128)(2,1)}) %all-gather.6.cloned.1.call-update) | async-done | bytes 14680080 | tf_op jit(solution)/shard_map/all_gather | solution.py:47
  207.2 95.6 %all-gather.8.cloned.1.call-done = bf16[1792,4096]{1,0:T(8,128)(2,1)} async-done(((bf16[1792,1024]{1,0:T(8,128)(2,1)}), bf16[1792,4096]{1,0:T(8,128)(2,1)}) %all-gather.8.cloned.1.call-update) | async-done | bytes 14680080 | tf_op jit(solution)/shard_map/all_gather | solution.py:51
  302.8 13.8 %fusion = bf16[1,128,4096]{2,1,0:T(8,128)(2,1)S(1)} fusion(bf16[1792,4096]{1,0:T(8,128)(2,1)} %all-gather.8.cloned.1.call-done, bf16[128,4096]{1,0:T(8,128)(2,1)S(1)} %bitcast.46, bf16[4096,1792]{1,0:T(8,128)(2,1)} %all-gather.6.cloned.1.call-done, f32[128,1792]{1,0:T(8,128)S(1)} %fusion.20, f32[1792]{0:T(1024)S(1)} %reduce), kind=kOutput, calls=%fused_computation.4 | convolution fusion | flops 3760226304 | bytes 32381952 | tf_op jit(solution)/shard_map/dot_general | solution.py:49
  316.6 2.4 copy.22
  319.0 0.0 copy-start.4
  319.0 0.0 copy-start.1
  319.0 0.5 broadcast.252
  319.5 7.2 %reduce.3 = bf16[128,4096]{1,0:T(8,128)(2,1)S(1)} reduce(bf16[128,1,4096]{2,1,0:T(2,128)(2,1)S(1)} %bitcast.47, bf16[]{:T(256)} %broadcast.252), dimensions={1}, to_apply=%bitcast.44.reduce_sub_computation | reduce | bytes 2097154
  326.8 1.6 reshape.253
  328.4 5.5 %all-to-all-start.2 = ((bf16[8,2,32768]{2,1,0:T(2,128)(2,1)}), bf16[8,2,32768]{2,1,0:T(2,128)(2,1)S(1)}, u32[]{:S(2)}, u32[]{:S(2)}) async-start(bf16[8,2,32768]{2,1,0:T(2,128)(2,1)} %reshape.253), calls=%async_computation.2 | async-start | bytes 2097152 | tf_op jit(solution)/shard_map/all_to_all | solution.py:80
  333.9 0.1 reshape.231
  334.0 26.1 %all-to-all-done.2 = bf16[8,2,32768]{2,1,0:T(2,128)(2,1)S(1)} async-done(((bf16[8,2,32768]{2,1,0:T(2,128)(2,1)}), bf16[8,2,32768]{2,1,0:T(2,128)(2,1)S(1)}, u32[]{:S(2)}, u32[]{:S(2)}) %all-to-all-start.2) | async-done | bytes 1048608 | tf_op jit(solution)/shard_map/all_to_all | solution.py:80
  360.1 1.0 reshape.254
  361.1 6.2 %bitcast_reduce_fusion = bf16[128,4096]{1,0:T(8,128)(2,1)S(1)} fusion(bf16[128,1,4096]{2,1,0:T(2,128)(2,1)S(1)} %reshape.254), kind=kLoop, calls=%fused_computation.52 | loop fusion | bytes 2097152 | tf_op jit(solution)/shard_map/all_to_all | solution.py:80
  367.3 0.4 reshape.230
  367.8 0.5 dynamic-slice_bitcast_fusion.3
  368.3 0.1 collective-permute-start.2
  368.4 0.7 collective-permute-start
  369.1 1.5 collective-permute-start.1
  370.5 6.4 %collective-permute-done.2 = bf16[1,8,4,4096]{3,2,1,0:T(4,128)(2,1)S(1)} collective-permute-done((bf16[1,8,4,4096]{3,2,1,0:T(4,128)(2,1)S(1)}, bf16[1,8,4,4096]{3,2,1,0:T(4,128)(2,1)S(1)}, u32[]{:S(2)}, u32[]{:S(2)}) %collective-permute-start.2) | collective-permute-done | bytes 262176 | tf_op jit(solution)/shard_map/ppermute | solution.py:98
  376.9 0.0 collective-permute-done
  376.9 4.4 %collective-permute-done.1 = bf16[1,8,4,4096]{3,2,1,0:T(4,128)(2,1)S(1)} collective-permute-done((bf16[1,8,4,4096]{3,2,1,0:T(4,128)(2,1)S(1)}, bf16[1,8,4,4096]{3,2,1,0:T(4,128)(2,1)S(1)}, u32[]{:S(2)}, u32[]{:S(2)}) %collective-permute-start.1) | collective-permute-done | bytes 262176 | tf_op jit(solution)/shard_map/ppermute | solution.py:98
  381.3 1.0 maximum_bitcast_fusion
  382.3 1.4 gather_fusion
  383.7 0.3 reshape_reshape.8
  384.0 0.9 gather_fusion.1
  384.9 1.1 multiply_reduce_fusion
  (12 shorter events, 0.1 us)
Async XLA Ops:
  6.5 4.1 %copy-start = (bf16[8,4096]{1,0:T(8,128)(2,1)S(1)}, bf16[8,4096]{1,0:T(8,128)(2,1)}, u32[]{:S(2)}) copy-start(bf16[8,4096]{1,0:T(8,128)(2,1)} %param.7) | copy-start | bytes 196612
  6.5 37.7 %copy-start.3 = (f32[1,1792]{1,0:T(1,128)S(1)}, f32[1,1792]{1,0:T(1,128)}, u32[]{:S(2)}) copy-start(f32[1,1792]{1,0:T(1,128)} %param.13) | copy-start | bytes 21508
  6.5 104.8 %all-gather.4.cloned.1.call-start = ((), (), s32[]{:S(2)}) async-start(), calls=%async_computation.3 | async-start | bytes 18350080 | tf_op jit(solution)/shard_map/all_gather | solution.py:46
  7.3 200.0 %all-gather.6.cloned.1.call-start = ((), (), s32[]{:S(2)}) async-start(), calls=%async_computation.4 | async-start | bytes 18350080 | tf_op jit(solution)/shard_map/all_gather | solution.py:47
  8.0 294.8 %all-gather.8.cloned.1.call-start = ((), (), s32[]{:S(2)}) async-start(), calls=%async_computation.5 | async-start | bytes 18350080 | tf_op jit(solution)/shard_map/all_gather | solution.py:51
  38.1 31.5 %all-to-all-start.1 = ((bf16[8,16,4096]{2,1,0:T(8,128)(2,1)}), bf16[8,16,4096]{2,1,0:T(8,128)(2,1)S(1)}, u32[]{:S(2)}, u32[]{:S(2)}) async-start(bf16[8,16,4096]{2,1,0:T(8,128)(2,1)} %copy.18), calls=%async_computation.1 | async-start | bytes 2097152 | tf_op jit(solution)/shard_map/all_to_all | solution.py:76
  118.5 215.3 %copy-start.2 = (s32[8,8]{1,0:T(8,128)S(1)}, s32[8,8]{1,0:T(8,128)}, u32[]{:S(2)}) copy-start(s32[8,8]{1,0:T(8,128)} %param.8) | copy-start | bytes 772
  319.0 65.9 %copy-start.4 = (f32[8,8]{1,0:T(8,128)S(1)}, f32[8,8]{1,0:T(8,128)}, u32[]{:S(2)}) copy-start(f32[8,8]{1,0:T(8,128)} %param.9) | copy-start | bytes 772
  319.0 67.0 %copy-start.1 = (bf16[8,4096]{1,0:T(8,128)(2,1)S(1)}, bf16[8,4096]{1,0:T(8,128)(2,1)}, u32[]{:S(2)}) copy-start(bf16[8,4096]{1,0:T(8,128)(2,1)} %param.7) | copy-start | bytes 196612
  328.4 31.7 %all-to-all-start.2 = ((bf16[8,2,32768]{2,1,0:T(2,128)(2,1)}), bf16[8,2,32768]{2,1,0:T(2,128)(2,1)S(1)}, u32[]{:S(2)}, u32[]{:S(2)}) async-start(bf16[8,2,32768]{2,1,0:T(2,128)(2,1)} %reshape.253), calls=%async_computation.2 | async-start | bytes 2097152 | tf_op jit(solution)/shard_map/all_to_all | solution.py:80
  368.3 8.6 %collective-permute-start.2 = (bf16[1,8,4,4096]{3,2,1,0:T(4,128)(2,1)S(1)}, bf16[1,8,4,4096]{3,2,1,0:T(4,128)(2,1)S(1)}, u32[]{:S(2)}, u32[]{:S(2)}) collective-permute-start(bf16[1,8,4,4096]{3,2,1,0:T(4,128)(2,1)S(1)} %get-tuple-element.8), channel_id=1, source_target_pairs={{0,24},{8,16},{16,8},{24,0},{1,25},{9,17},{17,9},{25,1},{2,26},{10... | collective-permute-start | bytes 786440 | tf_op jit(solution)/shard_map/ppermute | solution.py:98
  368.4 8.5 %collective-permute-start = (bf16[1,8,4,4096]{3,2,1,0:T(4,128)(2,1)S(1)}, bf16[1,8,4,4096]{3,2,1,0:T(4,128)(2,1)S(1)}, u32[]{:S(2)}, u32[]{:S(2)}) collective-permute-start(bf16[1,8,4,4096]{3,2,1,0:T(4,128)(2,1)S(1)} %get-tuple-element.10), channel_id=1, source_target_pairs={{0,8},{8,0},{16,24},{24,16},{1,9},{9,1},{17,25},{25,17},{2,10},{10... | collective-permute-start | bytes 786440 | tf_op jit(solution)/shard_map/ppermute | solution.py:98
  369.1 12.3 %collective-permute-start.1 = (bf16[1,8,4,4096]{3,2,1,0:T(4,128)(2,1)S(1)}, bf16[1,8,4,4096]{3,2,1,0:T(4,128)(2,1)S(1)}, u32[]{:S(2)}, u32[]{:S(2)}) collective-permute-start(bf16[1,8,4,4096]{3,2,1,0:T(4,128)(2,1)S(1)} %get-tuple-element.9), channel_id=1, source_target_pairs={{0,16},{8,24},{16,0},{24,8},{1,17},{9,25},{17,1},{25,9},{2,18},{10... | collective-permute-start | bytes 786440 | tf_op jit(solution)/shard_map/ppermute | solution.py:98
Sparse Core Ops, SparseCore 0:
  8.9 102.3 all-gather.3
  112.8 94.3 all-gather.5
  208.8 94.0 all-gather.7
